TPU v7x, 32 devices: a whole 2x2x4 slice. The times are simulated.
32 devices in a mesh: row: 4 (over x, core), col: 8 (over z, y).
Axes of the slice: x: 2, y: 2, z: 4, core: 2. Of those that a mesh axis runs over, the one named last changes fastest.
Arguments:
- amplitudes: float32 [262144, 1024], P(('row', 'col')), may hold values from -6 to 6
- integrals: float32 [262144, 1024], P(('row', 'col')), may hold values from -0.0234375 to 0.0234375
- denominators: float32 [1024, 1024], P('col', 'row'), may hold values from 1 to 4
- history: float32 [8, 1024, 1024], P(None, 'col', 'row'), may hold values from -80 to 80
Outputs:
- extrapolated: float32 [1024, 1024], P('col', 'row')
- coefficients: float32 [8], replicated
All inputs are finite; a program needn't handle non-finite values.
Results may differ from a plain program's by a relative error of at most 0.00005.
Values sent between devices are 32-bit elements; how exact they have to be, the bound alone decides.
A program may use at most 128 MiB of HBM per device.

v0:
```python
import jax
import jax.numpy as jnp
from jax import lax
from jax.sharding import PartitionSpec as P

OCC = 32
VBLK = 32


def weights_of(gram):
    count = gram.shape[0]
    ridge = 1e-06 * jnp.trace(gram) / count
    factor = jnp.linalg.cholesky(gram + ridge * jnp.eye(count, dtype=gram.dtype))
    ones = jnp.ones((count, 1), gram.dtype)
    half = lax.linalg.triangular_solve(factor, ones, left_side=True, lower=True)
    whole = lax.linalg.triangular_solve(factor, half, left_side=True, lower=True, transpose_a=True)
    return whole[:, 0] / jnp.sum(whole)


def shards(amplitudes, integrals, denominators, history):
    n_col = lax.axis_size("col")
    n_row = lax.axis_size("row")
    occ_group = OCC // n_col
    vir_group = VBLK // n_row
    pair_rows = lax.psum_scatter(
        lax.dot_general(
            amplitudes,
            integrals,
            (((0,), (0,)), ((), ())),
            precision=lax.Precision.HIGHEST,
            preferred_element_type=jnp.float32,
        ),
        "col",
        scatter_dimension=0,
        tiled=True,
    )
    block = lax.psum_scatter(pair_rows, "row", scatter_dimension=1, tiled=True)
    shaped = block.reshape(occ_group, n_col, occ_group, vir_group, n_row, vir_group)
    swapped = lax.all_to_all(
        lax.all_to_all(shaped, "row", split_axis=4, concat_axis=4, tiled=True),
        "col",
        split_axis=1,
        concat_axis=1,
        tiled=True,
    )
    mirror_part = swapped.transpose(2, 1, 0, 5, 4, 3).reshape(block.shape)
    symmetric = block + mirror_part
    update = symmetric / denominators
    following = jnp.concatenate([history[1:], update[None]], axis=0)
    errors = following - history
    gram = lax.psum(
        jnp.einsum("kxy,lxy->kl", errors, errors, precision=lax.Precision.HIGHEST), ("row", "col")
    )
    coefficients = weights_of(gram)
    extrapolated = jnp.einsum("k,kxy->xy", coefficients, following, precision=lax.Precision.HIGHEST)
    return (extrapolated, coefficients)


def solution(mesh):
    return jax.shard_map(
        shards,
        mesh=mesh,
        in_specs=(
            P(("row", "col"), None),
            P(("row", "col"), None),
            P("col", "row"),
            P(None, "col", "row"),
        ),
        out_specs=(P("col", "row"), P()),
        check_vma=False,
    )
```

profile of v0, /device:TPU:0, one launch (start us, length us, event | category | flops | bytes accessed | tf_op | source)
XLA Modules:
  0.0 336.2 jit_solution(11061221960056895199)
XLA Ops:
  7.2 0.0 reduce-scatter.3.cloned.1.call-start
  7.2 113.4 %fusion.11 = f32[1024,1024]{1,0:T(8,128)} fusion(f32[8192,1024]{1,0:T(8,128)} %param.4, f32[8192,1024]{1,0:T(8,128)} %param.5), kind=kOutput, calls=%fused_computation.28 | convolution fusion | flops 103079215104 | bytes 71303168 | tf_op jit(solution)/shard_map/dot_general | solution.py:26
  120.6 0.0 reduce-scatter.3.cloned.1.call-update
  120.6 0.0 reduce-scatter.5.cloned.1.call-start
  120.7 90.7 %reduce-scatter.3.cloned.1.call-done = f32[128,1024]{1,0:T(8,128)} async-done(((f32[1024,1024]{1,0:T(8,128)}), f32[128,1024]{1,0:T(8,128)}) %reduce-scatter.3.cloned.1.call-update) | async-done | bytes 524304 | tf_op jit(solution)/shard_map/reduce_scatter | solution.py:25
  211.4 0.0 reduce-scatter.5.cloned.1.call-update
  211.4 24.0 %reduce-scatter.5.cloned.1.call-done = f32[128,256]{1,0:T(8,128)} async-done(((f32[128,1024]{1,0:T(8,128)}), f32[128,256]{1,0:T(8,128)}) %reduce-scatter.5.cloned.1.call-update) | async-done | bytes 131088 | tf_op jit(solution)/shard_map/reduce_scatter | solution.py:37
  235.5 4.7 %reshape.28 = f32[4,8,4,8,4,8]{5,4,3,2,1,0:T(4,128)} reshape(f32[128,256]{1,0:T(8,128)} %reduce-scatter.5.cloned.1.call-done) | data formatting | bytes 262144 | tf_op jit(solution)/shard_map/reshape | solution.py:38
  240.2 1.9 copy.15
  242.2 1.1 reshape.37
  243.2 7.0 %all_to_all.10 = f32[4,1,8192]{2,1,0:T(1,128)S(1)} all-to-all(f32[4,1,8192]{2,1,0:T(1,128)S(1)} %reshape.37), channel_id=1, replica_groups=mesh['row'=4,'col'=8] {'row'}, dimensions={0} | all-to-all | bytes 262144 | tf_op jit(solution)/shard_map/all_to_all | solution.py:40
  250.3 0.5 broadcast.71
  250.8 1.0 reduce.8
  251.7 1.1 reshape.38
  252.9 3.1 copy.37
  256.0 4.7 %reshape.39 = f32[8,1,4096]{2,1,0:T(1,128)} reshape(f32[8,4,4,8,4,8]{5,4,3,2,1,0:T(4,128)} %bitcast.43) | data formatting | bytes 262144
  260.7 5.5 %all-to-all-start.1 = ((f32[8,1,4096]{2,1,0:T(1,128)}), f32[8,1,4096]{2,1,0:T(1,128)S(1)}, u32[]{:S(2)}, u32[]{:S(2)}) async-start(f32[8,1,4096]{2,1,0:T(1,128)} %reshape.39), calls=%async_computation.3 | async-start | bytes 262144 | tf_op jit(solution)/shard_map/all_to_all | solution.py:39
  266.2 7.3 %all-to-all-done.1 = f32[8,1,4096]{2,1,0:T(1,128)S(1)} async-done(((f32[8,1,4096]{2,1,0:T(1,128)}), f32[8,1,4096]{2,1,0:T(1,128)S(1)}, u32[]{:S(2)}, u32[]{:S(2)}) %all-to-all-start.1) | async-done | bytes 131104 | tf_op jit(solution)/shard_map/all_to_all | solution.py:39
  273.6 1.0 reduce.9
  274.5 2.5 reshape.40
  277.0 0.2 bitcast_bitcast_fusion
  277.2 0.0 copy-start
  277.2 0.0 copy-start.1
  277.2 0.0 slice-start
  277.2 0.2 copy.17
  277.4 2.4 reshape.29
  279.8 0.0 copy-done
  279.9 0.0 copy-done.1
  279.9 0.0 slice-done
  279.9 1.4 fusion.9
  281.3 2.5 convolution_bitcast_fusion
  283.8 37.6 %psum.7 = f32[8,8]{0,1:T(8,128)S(1)} all-reduce(f32[8,8]{0,1:T(8,128)S(1)} %convolution_bitcast_fusion), channel_id=1, replica_groups=mesh['row'=4,'col'=8] {'row','col'}, use_global_device_ids=true, to_apply=%region_2.0 | all-reduce | flops 64 | bytes 512 | tf_op jit(solution)/shard_map/psum | solution.py:51
  321.3 0.6 select_reduce_fusion.1
  322.6 0.1 copy.21
  322.7 0.7 cholesky.17
  323.4 0.1 copy.22
  323.5 0.1 select_reduce_fusion
  323.6 0.6 compare_reduce_fusion
  324.3 0.6 select_select_fusion
  324.9 0.1 copy.24
  325.0 0.6 custom-call.8
  325.6 0.1 convolution_bitcast_fusion.2
  325.7 0.8 fusion.10
  326.5 0.6 broadcast_divide_fusion
  327.1 0.0 copy-start.2
  327.2 1.5 fusion
  328.6 0.7 copy.36
  329.3 0.0 copy-done.2
  (3 shorter events, 0.0 us)
Async XLA Ops:
  7.2 204.3 %reduce-scatter.3.cloned.1.call-start = ((), (), s32[]{:S(2)}) async-start(), calls=%async_computation.4 | async-start | bytes 4718592 | tf_op jit(solution)/shard_map/reduce_scatter | solution.py:25
  120.6 114.8 %reduce-scatter.5.cloned.1.call-start = ((), (), s32[]{:S(2)}) async-start(), calls=%async_computation.5 | async-start | bytes 655360 | tf_op jit(solution)/shard_map/reduce_scatter | solution.py:37
  260.7 12.9 %all-to-all-start.1 = ((f32[8,1,4096]{2,1,0:T(1,128)}), f32[8,1,4096]{2,1,0:T(1,128)S(1)}, u32[]{:S(2)}, u32[]{:S(2)}) async-start(f32[8,1,4096]{2,1,0:T(1,128)} %reshape.39), calls=%async_computation.3 | async-start | bytes 262144 | tf_op jit(solution)/shard_map/all_to_all | solution.py:39
  277.2 2.7 copy-start
  277.2 2.7 copy-start.1
  277.2 2.7 slice-start
  327.1 2.2 copy-start.2
Sparse Core Ops, SparseCore 0:
  120.8 90.6 reduce-scatter.2
  214.1 21.3 reduce-scatter.4
where the time goes:
time: 337 us; the launch traced here: 336 us
  waiting for transfers between devices  122 us (36%)
  matrix products  118 us (35%)
  blocking collectives  44.6 us (13%)
  local copies, waits for them, and re-layouts  23.4 us (7%)
  between operations  14.8 us (4%)
  other arithmetic  7.36 us (2%)
  starting transfers between devices  5.59 us (2%)
    dot_general x1, matrix products, shards(): lax.dot_general(amplitudes, integrals, (((0,), (0,)), ((), ())), precisio...  113 us
    reduce_scatter x1, waiting for transfers between devices, shards(): lax.psum_scatter(lax.dot_general(amplitudes, integrals, (((0,), (0,)), ((...  90.7 us
    psum x1, blocking collectives, shards(): lax.psum(jnp.einsum('kxy,lxy->kl', errors, errors, precision=lax.Precisio...  37.6 us
    reduce_scatter x1, waiting for transfers between devices, shards(): block = lax.psum_scatter(pair_rows, 'row', scatter_dimension=1, tiled=True)  24 us
    unnamed x10, local copies, waits for them, and re-layouts  9.37 us
    all_to_all x1, waiting for transfers between devices, shards(): lax.all_to_all(lax.all_to_all(shaped, 'row', split_axis=4, concat_axis=4,...  7.34 us
    all_to_all x1, blocking collectives, shards(): lax.all_to_all(shaped, 'row', split_axis=4, concat_axis=4, tiled=True)  7.02 us
  transfers between devices with their start and end apart: 3, of which 3 were waited for; matrix products, arithmetic and copies ran while one was open for 0% of the time, Pallas kernels for 0%

commit v1 on v0

--- a/solution.py
+++ b/solution.py
@@ -1,10 +1,262 @@
+import functools
+
 import jax
 import jax.numpy as jnp
 from jax import lax
+from jax.experimental import pallas as pl
+from jax.experimental.pallas import tpu as pltpu
 from jax.sharding import PartitionSpec as P
 
 OCC = 32
 VBLK = 32
+MESH = pl.DeviceIdType.MESH
+F32 = jnp.float32
+BF16 = jnp.bfloat16
+SLOTS = 3
+MIB = 1 << 20
+
+
+def ring_place(row, n_row):
+    return jnp.where(lax.rem(row, 2) == 0, row // 2, n_row - 1 - row // 2)
+
+
+def ring_row(place, n_row):
+    return jnp.where(place < n_row // 2, 2 * place, 2 * (n_row - 1 - place) + 1)
+
+
+def two_parts(x):
+    high = x.astype(BF16)
+    return high, (x - high.astype(F32)).astype(BF16)
+
+
+def dot(a, b):
+    return jnp.dot(a, b, preferred_element_type=F32)
+
+
+def ladder_kernel(
+    n_row, n_col, n_sub, kb,
+    t_hbm, v_hbm, out_ref,
+    t_high, t_low, v_high, v_low, t_stage, v_stage, first, ring, pair, line,
+    t_sem, v_sem, ring_send, ring_recv, pair_send, pair_recv, line_send, line_recv,
+):
+    depth, pairs = t_hbm.shape
+    width = v_hbm.shape[1] // n_row
+    rows = pairs // n_col
+    q = rows // n_sub
+    sub = n_col * q
+    half = sub // 2
+    n_line = n_col // 2
+    blocks = depth // kb
+    per_sub = blocks // n_sub
+    kc = kb * n_sub
+    row = lax.axis_index("row")
+    col = lax.axis_index("col")
+    place = ring_place(row, n_row)
+    after = ring_row(lax.rem(place + 1, n_row), n_row)
+    before = ring_row(lax.rem(place + n_row - 1, n_row), n_row)
+    side = lax.rem(col, 2)
+    along = col // 2
+    other = along * 2 + 1 - side
+
+    def line_col(k):
+        return lax.rem(along + k, n_line) * 2 + side
+
+    barrier = pltpu.get_barrier_semaphore()
+    peers = [(after, col), (before, col), (row, other)]
+    peers += [(row, line_col(k)) for k in range(1, n_line)]
+    for peer in peers:
+        pl.semaphore_signal(barrier, inc=1, device_id=peer, device_id_type=MESH)
+
+    def columns(step):
+        owner = ring_row(lax.rem(place - 1 - step + 2 * n_row, n_row), n_row)
+        return pl.ds(pl.multiple_of(owner * width, width), width)
+
+    def t_copy(b):
+        slot = lax.rem(b, SLOTS)
+        at = pl.multiple_of(b * kb, kb)
+        return pltpu.make_async_copy(t_hbm.at[pl.ds(at, kb), :], t_stage.at[slot], t_sem.at[slot])
+
+    def v_copy(step, b):
+        slot = lax.rem(b, SLOTS)
+        at = pl.multiple_of(b * kb, kb)
+        return pltpu.make_async_copy(
+            v_hbm.at[pl.ds(at, kb), columns(step)],
+            v_stage.at[step % 2, slot],
+            v_sem.at[step % 2, slot],
+        )
+
+    def keep_v(step, b):
+        at = pl.multiple_of(b * kb, kb)
+        high, low = two_parts(v_stage[step % 2, lax.rem(b, SLOTS)])
+        v_high[step % 2, pl.ds(at, kb), :] = high
+        v_low[step % 2, pl.ds(at, kb), :] = low
+        return high, low
+
+    def ring_copy(step, m):
+        source = first if step == 0 else ring.at[step - 1]
+        return pltpu.make_async_remote_copy(
+            source.at[m], ring.at[step, m],
+            ring_send.at[step, m], ring_recv.at[step, m],
+            device_id=(after, col), device_id_type=MESH,
+        )
+
+    def pair_copy(m):
+        at = pl.multiple_of((1 - side) * half, half)
+        return pltpu.make_async_remote_copy(
+            ring.at[n_row - 2, m, pl.ds(at, half), :], pair.at[m],
+            pair_send.at[m], pair_recv.at[m],
+            device_id=(row, other), device_id_type=MESH,
+        )
+
+    def line_copy(m, k):
+        at = pl.multiple_of(lax.rem(along + k, n_line) * q, q)
+        return pltpu.make_async_remote_copy(
+            pair.at[m, pl.ds(at, q), :], line.at[m, k - 1],
+            line_send.at[m, k - 1], line_recv.at[m, k - 1],
+            device_id=(row, line_col(k)), device_id_type=MESH,
+        )
+
+    for b in range(SLOTS):
+        t_copy(b).start()
+        v_copy(0, b).start()
+        v_copy(1, b).start()
+    first[...] = jnp.zeros_like(first)
+
+    def load(b, carry):
+        t_copy(b).wait()
+        v_copy(0, b).wait()
+        v_copy(1, b).wait()
+        at = pl.multiple_of(b * kb, kb)
+        vh, vl = keep_v(0, b)
+        keep_v(1, b)
+        slot = lax.rem(b, SLOTS)
+        for c in range(n_col):
+            turned = t_stage[slot, :, c * rows:(c + 1) * rows].T
+            th, tl = two_parts(turned)
+            for m in range(n_sub):
+                to = m * sub + ((c % 2) * n_line + c // 2) * q
+                t_high[to:to + q, pl.ds(at, kb)] = th[m * q:(m + 1) * q]
+                t_low[to:to + q, pl.ds(at, kb)] = tl[m * q:(m + 1) * q]
+
+        @pl.when(b + SLOTS < blocks)
+        def _():
+            t_copy(b + SLOTS).start()
+            v_copy(0, b + SLOTS).start()
+            v_copy(1, b + SLOTS).start()
+
+        for m in range(n_sub):
+            th = t_high[m * sub:(m + 1) * sub, pl.ds(at, kb)]
+            tl = t_low[m * sub:(m + 1) * sub, pl.ds(at, kb)]
+            first[m] += dot(th, vh) + dot(th, vl) + dot(tl, vh)
+        return carry
+
+    lax.fori_loop(0, blocks, load, 0)
+
+    pl.semaphore_wait(barrier, len(peers))
+    for b in range(SLOTS):
+        v_copy(2, b).start()
+    for m in range(n_sub):
+        ring_copy(0, m).start()
+
+    def spread(m):
+        pair_copy(m).wait_recv()
+        at = pl.multiple_of(side * half, half)
+        pair[m] += ring[n_row - 2, m, pl.ds(at, half), :]
+        for k in range(1, n_line):
+            line_copy(m, k).start()
+
+    for step in range(1, n_row):
+        if step + 2 < n_row:
+            for b in range(SLOTS):
+                v_copy(step + 2, b).start()
+        for m in range(n_sub):
+            first_rows = slice(m * sub, (m + 1) * sub)
+            ring_copy(step - 1, m).wait_recv()
+
+            def more(i, carry, step=step, m=m, first_rows=first_rows):
+                if step < n_row - 1:
+                    b = m * per_sub + i
+                    v_copy(step + 1, b).wait()
+                    keep_v(step + 1, b)
+
+                    @pl.when(b + SLOTS < blocks)
+                    def _():
+                        v_copy(step + 1, b + SLOTS).start()
+
+                at = pl.ds(pl.multiple_of(i * kc, kc), kc)
+                th = t_high[first_rows, at]
+                tl = t_low[first_rows, at]
+                vh = v_high[step % 2, at, :]
+                vl = v_low[step % 2, at, :]
+                ring[step - 1, m] += dot(th, vh) + dot(th, vl) + dot(tl, vh)
+                return carry
+
+            lax.fori_loop(0, per_sub, more, 0)
+            if step < n_row - 1:
+                ring_copy(step, m).start()
+            else:
+                pair_copy(m).start()
+                if m > 0:
+                    spread(m - 1)
+    spread(n_sub - 1)
+    for m in range(n_sub):
+        mine = pair[m, pl.ds(pl.multiple_of(along * q, q), q), :]
+        for k in range(1, n_line):
+            line_copy(m, k).wait_recv()
+            mine += line[m, k - 1]
+        out_ref[m * q:(m + 1) * q, :] = mine
+    for m in range(n_sub):
+        for step in range(n_row - 1):
+            ring_copy(step, m).wait_send()
+        pair_copy(m).wait_send()
+        for k in range(1, n_line):
+            line_copy(m, k).wait_send()
+
+
+def ladder_block(amplitudes, integrals):
+    n_col = lax.axis_size("col")
+    n_row = lax.axis_size("row")
+    depth, pairs = amplitudes.shape
+    width = integrals.shape[1] // n_row
+    rows = pairs // n_col
+    n_sub = min(4, rows // 16)
+    kb = min(256, depth // n_sub)
+    q = rows // n_sub
+    sub = n_col * q
+    n_line = n_col // 2
+    dma = pltpu.SemaphoreType.DMA
+    return pl.pallas_call(
+        functools.partial(ladder_kernel, n_row, n_col, n_sub, kb),
+        out_shape=jax.ShapeDtypeStruct((rows, width), F32),
+        in_specs=[pl.BlockSpec(memory_space=pl.ANY)] * 2,
+        out_specs=pl.BlockSpec(memory_space=pltpu.VMEM),
+        scratch_shapes=[
+            pltpu.VMEM((pairs, depth), BF16),
+            pltpu.VMEM((pairs, depth), BF16),
+            pltpu.VMEM((2, depth, width), BF16),
+            pltpu.VMEM((2, depth, width), BF16),
+            pltpu.VMEM((SLOTS, kb, pairs), F32),
+            pltpu.VMEM((2, SLOTS, kb, width), F32),
+            pltpu.VMEM((n_sub, sub, width), F32),
+            pltpu.VMEM((n_row - 1, n_sub, sub, width), F32),
+            pltpu.VMEM((n_sub, sub // 2, width), F32),
+            pltpu.VMEM((n_sub, n_line - 1, q, width), F32),
+            dma((SLOTS,)),
+            dma((2, SLOTS)),
+            dma((n_row - 1, n_sub)),
+            dma((n_row - 1, n_sub)),
+            dma((n_sub,)),
+            dma((n_sub,)),
+            dma((n_sub, n_line - 1)),
+            dma((n_sub, n_line - 1)),
+        ],
+        compiler_params=pltpu.CompilerParams(
+            collective_id=0, has_side_effects=True, vmem_limit_bytes=60 * MIB
+        ),
+        cost_estimate=pl.CostEstimate(
+            flops=6 * depth * pairs * pairs, bytes_accessed=8 * depth * pairs, transcendentals=0
+        ),
+    )(amplitudes, integrals)
 
 
 def weights_of(gram):
@@ -22,19 +274,7 @@
     n_row = lax.axis_size("row")
     occ_group = OCC // n_col
     vir_group = VBLK // n_row
-    pair_rows = lax.psum_scatter(
-        lax.dot_general(
-            amplitudes,
-            integrals,
-            (((0,), (0,)), ((), ())),
-            precision=lax.Precision.HIGHEST,
-            preferred_element_type=jnp.float32,
-        ),
-        "col",
-        scatter_dimension=0,
-        tiled=True,
-    )
-    block = lax.psum_scatter(pair_rows, "row", scatter_dimension=1, tiled=True)
+    block = ladder_block(amplitudes, integrals)
     shaped = block.reshape(occ_group, n_col, occ_group, vir_group, n_row, vir_group)
     swapped = lax.all_to_all(
         lax.all_to_all(shaped, "row", split_axis=4, concat_axis=4, tiled=True),

time: 337 us -> 198 us (0.59)
  waiting for transfers between devices: 122 us -> 7.28 us
  matrix products: 118 us -> 4.86 us
  Pallas kernels: 0 us -> 101 us
  between operations: 14.8 us -> 1.45 us
  blocking collectives: 44.6 us -> 48.8 us
    reduce_scatter x2 -> x0, waiting for transfers between devices: 115 us -> none  [the longest x1 90.7 us: shards(): lax.psum_scatter(lax.dot_general(amplitudes, integrals, (((0,), (0,)), ((...]
    dot_general x1 -> x0, matrix products: 113 us -> none  [shards(): lax.dot_general(amplitudes, integrals, (((0,), (0,)), ((), ())), precisio...]
    pallas_call x0 -> x1, Pallas kernels: none -> 101 us  [ladder_block(): pl.pallas_call(functools.partial(ladder_kernel, n_row, n_col, n_sub, kb),...]
    all_to_all x1, blocking collectives: 7.02 us -> 11 us  [shards(): lax.all_to_all(shaped, 'row', split_axis=4, concat_axis=4, tiled=True)]
  transfers between devices with their start and end apart: 3 -> 1, of which waited for: 3 -> 1; matrix products, arithmetic and copies ran while one was open for 0% -> 0% of each run, Pallas kernels for 0% -> 0%
where the time goes in v1:
time: 198 us
  Pallas kernels  101 us (51%)
  blocking collectives  48.8 us (25%)
  local copies, waits for them, and re-layouts  23.4 us (12%)
  other arithmetic  7.36 us (4%)
  waiting for transfers between devices  7.28 us (4%)
  matrix products  4.86 us (2%)
  starting transfers between devices  3.37 us (2%)
    pallas_call x1, Pallas kernels, ladder_block(): pl.pallas_call(functools.partial(ladder_kernel, n_row, n_col, n_sub, kb),...  101 us
    psum x1, blocking collectives, shards(): lax.psum(jnp.einsum('kxy,lxy->kl', errors, errors, precision=lax.Precisio...  37.8 us
    all_to_all x1, blocking collectives, shards(): lax.all_to_all(shaped, 'row', split_axis=4, concat_axis=4, tiled=True)  11 us
    unnamed x10, local copies, waits for them, and re-layouts  9.37 us
    all_to_all x1, waiting for transfers between devices, shards(): lax.all_to_all(lax.all_to_all(shaped, 'row', split_axis=4, concat_axis=4,...  7.28 us
    reshape x2, local copies, waits for them, and re-layouts, shards(): block.reshape(occ_group, n_col, occ_group, vir_group, n_row, vir_group)  6.67 us
  transfers between devices with their start and end apart: 1, of which 1 were waited for; matrix products, arithmetic and copies ran while one was open for 0% of the time, Pallas kernels for 0%

profile of v1, /device:TPU:0, one launch (start us, length us, event | category | flops | bytes accessed | tf_op | source)
XLA Modules:
  0.0 197.6 jit_solution(18174064062773406882)
XLA Ops:
  0.6 101.1 %shard_map.59 = f32[128,256]{1,0:T(8,128)} custom-call(f32[8192,1024]{1,0:T(8,128)} %t_hbm.1, f32[8192,1024]{1,0:T(8,128)} %v_hbm.1), custom_call_target="tpu_custom_call" | custom-call | flops 51539607552 | bytes 67108864 | tf_op jit(solution)/shard_map/pallas_call | solution.py:228
  101.8 4.7 %reshape.28 = f32[4,8,4,8,4,8]{5,4,3,2,1,0:T(4,128)} reshape(f32[128,256]{1,0:T(8,128)} %shard_map.59) | data formatting | bytes 262144 | tf_op jit(solution)/shard_map/reshape | solution.py:278
  106.5 1.9 copy.15
  108.5 1.1 reshape.37
  109.5 11.0 %all_to_all.10 = f32[4,1,8192]{2,1,0:T(1,128)S(1)} all-to-all(f32[4,1,8192]{2,1,0:T(1,128)S(1)} %reshape.37), channel_id=1, replica_groups=mesh['row'=4,'col'=8] {'row'}, dimensions={0} | all-to-all | bytes 262144 | tf_op jit(solution)/shard_map/all_to_all | solution.py:280
  120.5 0.5 broadcast.71
  121.0 1.0 reduce.8
  122.0 1.1 reshape.38
  123.1 3.1 %copy.37 = f32[4,8,4,8,4,8]{3,4,5,0,2,1:T(4,128)} copy(f32[4,8,4,8,4,8]{3,5,0,1,2,4:T(8,128)S(1)} %bitcast.40) | data formatting | bytes 262144 | tf_op jit(solution)/shard_map/all_to_all | solution.py:280
  126.3 4.7 %reshape.39 = f32[8,1,4096]{2,1,0:T(1,128)} reshape(f32[8,4,4,8,4,8]{5,4,3,2,1,0:T(4,128)} %bitcast.41) | data formatting | bytes 262144
  131.0 3.4 %all-to-all-start.1 = ((f32[8,1,4096]{2,1,0:T(1,128)}), f32[8,1,4096]{2,1,0:T(1,128)S(1)}, u32[]{:S(2)}, u32[]{:S(2)}) async-start(f32[8,1,4096]{2,1,0:T(1,128)} %reshape.39), calls=%async_computation.1 | async-start | bytes 262144 | tf_op jit(solution)/shard_map/all_to_all | solution.py:279
  134.3 7.3 %all-to-all-done.1 = f32[8,1,4096]{2,1,0:T(1,128)S(1)} async-done(((f32[8,1,4096]{2,1,0:T(1,128)}), f32[8,1,4096]{2,1,0:T(1,128)S(1)}, u32[]{:S(2)}, u32[]{:S(2)}) %all-to-all-start.1) | async-done | bytes 131104 | tf_op jit(solution)/shard_map/all_to_all | solution.py:279
  141.6 1.0 reduce.9
  142.6 2.5 %reshape.40 = f32[8,4,4,8,4,8]{5,4,3,2,1,0:T(4,128)S(1)} reshape(f32[8,4096]{1,0:T(8,128)S(1)} %reduce.9) | data formatting | bytes 262144
  145.1 0.2 bitcast_bitcast_fusion
  145.3 0.2 copy.17
  145.4 0.0 copy-start
  145.4 0.0 copy-start.1
  145.5 0.0 slice-start
  145.5 2.4 %reshape.29 = f32[128,256]{1,0:T(8,128)S(1)} reshape(f32[4,8,4,8,4,8]{5,4,3,2,1,0:T(4,128)S(1)} %copy.17) | data formatting | bytes 262144 | tf_op jit(solution)/shard_map/reshape | solution.py:286
  147.9 0.0 copy-done
  147.9 0.0 copy-done.1
  148.0 0.0 slice-done
  148.0 1.4 fusion.9
  149.3 2.5 %convolution_bitcast_fusion = f32[8,8]{0,1:T(8,128)S(1)} fusion(f32[8,128,256]{2,1,0:T(8,128)S(1)} %get-tuple-element.2), kind=kOutput, calls=%fused_computation | convolution fusion | flops 25165824 | bytes 1048832 | tf_op jit(solution)/shard_map/kxy,lxy->kl/dot_general | solution.py:292
  151.8 37.8 %psum.7 = f32[8,8]{0,1:T(8,128)S(1)} all-reduce(f32[8,8]{0,1:T(8,128)S(1)} %convolution_bitcast_fusion), channel_id=1, replica_groups=mesh['row'=4,'col'=8] {'row','col'}, use_global_device_ids=true, to_apply=%region_0.0 | all-reduce | flops 64 | bytes 512 | tf_op jit(solution)/shard_map/psum | solution.py:291
  189.6 0.6 select_reduce_fusion.1
  190.9 0.1 copy.21
  191.0 0.7 cholesky.17
  191.7 0.1 copy.22
  191.7 0.1 select_reduce_fusion
  191.9 0.6 compare_reduce_fusion
  192.5 0.6 select_select_fusion
  193.2 0.1 copy.24
  193.3 0.6 custom-call.8
  193.9 0.1 convolution_bitcast_fusion.2
  194.0 0.8 fusion.10
  194.8 0.6 broadcast_divide_fusion
  195.4 0.0 copy-start.2
  195.4 1.5 fusion
  196.9 0.7 copy.36
  197.6 0.0 copy-done.2
  (3 shorter events, 0.0 us)
Async XLA Ops:
  131.0 10.7 %all-to-all-start.1 = ((f32[8,1,4096]{2,1,0:T(1,128)}), f32[8,1,4096]{2,1,0:T(1,128)S(1)}, u32[]{:S(2)}, u32[]{:S(2)}) async-start(f32[8,1,4096]{2,1,0:T(1,128)} %reshape.39), calls=%async_computation.1 | async-start | bytes 262144 | tf_op jit(solution)/shard_map/all_to_all | solution.py:279
  145.4 2.5 %copy-start = (f32[128,256]{1,0:T(8,128)S(1)}, f32[128,256]{1,0:T(8,128)}, u32[]{:S(2)}) copy-start(f32[128,256]{1,0:T(8,128)} %shard_map.59) | copy-start | bytes 393220
  145.4 2.5 %copy-start.1 = (f32[128,256]{1,0:T(8,128)S(1)}, f32[128,256]{1,0:T(8,128)}, u32[]{:S(2)}) copy-start(f32[128,256]{1,0:T(8,128)} %param.6) | copy-start | bytes 393220
  145.5 2.5 %slice-start = ((f32[8,128,256]{2,1,0:T(8,128)}), f32[7,128,256]{2,1,0:T(8,128)S(1)}, s32[]{:S(2)}) async-start(f32[8,128,256]{2,1,0:T(8,128)} %param.7), calls=%async_computation.2 | async-start | bytes 1835008 | tf_op jit(solution)/shard_map/slice | solution.py:289
  195.4 2.2 %copy-start.2 = (f32[8]{0:T(128)}, f32[8]{0:T(128)S(1)}, u32[]{:S(2)}) copy-start(f32[8]{0:T(128)S(1)} %broadcast_divide_fusion) | copy-start | bytes 100

commit v2 on v1

--- a/solution.py
+++ b/solution.py
@@ -259,41 +259,177 @@
     )(amplitudes, integrals)
 
 
-def weights_of(gram):
-    count = gram.shape[0]
-    ridge = 1e-06 * jnp.trace(gram) / count
-    factor = jnp.linalg.cholesky(gram + ridge * jnp.eye(count, dtype=gram.dtype))
-    ones = jnp.ones((count, 1), gram.dtype)
-    half = lax.linalg.triangular_solve(factor, ones, left_side=True, lower=True)
-    whole = lax.linalg.triangular_solve(factor, half, left_side=True, lower=True, transpose_a=True)
-    return whole[:, 0] / jnp.sum(whole)
-
-
-def shards(amplitudes, integrals, denominators, history):
+def exact(a, b):
+    return jnp.dot(a, b, precision=lax.Precision.HIGHEST, preferred_element_type=F32)
+
+
+def finish_kernel(
+    n_row, n_col, group, lanes,
+    block_ref, den_ref, hist_ref, out_ref, coef_ref,
+    packed, landed, grams, send_sem, recv_sem, gram_send, gram_recv,
+):
+    count = hist_ref.shape[0]
+    rows, width = block_ref.shape
+    og = OCC // n_col
+    vg = VBLK // n_row
+    n = n_row * n_col
+    row = lax.axis_index("row")
+    col = lax.axis_index("col")
+    me = row * n_col + col
+
+    def peer(k):
+        to = lax.rem(me + k, n)
+        return to // n_col, lax.rem(to, n_col)
+
+    def spot(of_row, of_col):
+        return (
+            pl.ds(pl.multiple_of(of_col * group, group), group),
+            pl.ds(pl.multiple_of(of_row * lanes, lanes), lanes),
+        )
+
+    def mirror_copy(k, target):
+        to_row, to_col = peer(k)
+        return pltpu.make_async_remote_copy(
+            packed.at[spot(to_row, to_col)], landed.at[target],
+            send_sem.at[k - 1], recv_sem.at[k - 1],
+            device_id=(to_row, to_col), device_id_type=MESH,
+        )
+
+    def gram_copy(k, slot):
+        return pltpu.make_async_remote_copy(
+            grams.at[me], grams.at[slot],
+            gram_send.at[k - 1], gram_recv.at[k - 1],
+            device_id=peer(k), device_id_type=MESH,
+        )
+
+    def each(body):
+        def step(k, carry):
+            body(k)
+            return carry
+
+        lax.fori_loop(1, n, step, 0)
+
+    barrier = pltpu.get_barrier_semaphore()
+    each(lambda k: pl.semaphore_signal(barrier, inc=1, device_id=peer(k), device_id_type=MESH))
+
+    def iota(shape, axis):
+        return lax.broadcasted_iota(jnp.int32, shape, axis)
+
+    def hot(hits):
+        return jnp.where(hits, 1.0, 0.0).astype(F32)
+
+    shape = (n_col * group, rows)
+    at = iota(shape, 1)
+    j = at % OCC
+    take_rows = hot(iota(shape, 0) == (j // og) * group + (at // OCC) * og + j % og)
+    shape = (width, n_row * lanes)
+    at = iota(shape, 0)
+    b = at % VBLK
+    take_lanes = hot(iota(shape, 1) == (b // vg) * lanes + (at // VBLK) * vg + b % vg)
+    packed[...] = exact(exact(take_rows, block_ref[...]), take_lanes)
+    landed[spot(row, col)] = packed[spot(row, col)]
+
+    pl.semaphore_wait(barrier, n - 1)
+    each(lambda k: mirror_copy(k, spot(row, col)).start())
+
+    shape = (rows, n_col * group)
+    at = iota(shape, 0)
+    i = at % OCC
+    give_rows = hot(iota(shape, 1) == (i // og) * group + (i % og) * og + at // OCC)
+    shape = (n_row * lanes, width)
+    at = iota(shape, 1)
+    a = at % VBLK
+    give_lanes = hot(iota(shape, 0) == (a // vg) * lanes + (a % vg) * vg + at // VBLK)
+
+    tile = (count, 128)
+    down = iota(tile, 0)
+    over = iota(tile, 1)
+
+    def place(total, k, l, x, y):
+        value = jnp.sum(jnp.sum(x * y, axis=0, keepdims=True), axis=1, keepdims=True)
+        hits = ((down == k) & (over == l)) | ((down == l) & (over == k))
+        return jnp.where(hits, value, total)
+
+    def step_of(k):
+        return hist_ref[k + 1] - hist_ref[k]
+
+    gram = jnp.zeros(tile, F32)
+    for k in range(count - 1):
+        for l in range(k, count - 1):
+            gram = place(gram, k, l, step_of(k), step_of(l))
+
+    def arrive(k):
+        source = lax.rem(me + n - k, n)
+        mirror_copy(k, spot(source // n_col, lax.rem(source, n_col))).wait_recv()
+
+    each(arrive)
+    symmetric = block_ref[...] + exact(exact(give_rows, landed[...]), give_lanes)
+    update = symmetric / den_ref[...]
+    out_ref[...] = update
+    last = update - hist_ref[count - 1]
+    for k in range(count - 1):
+        gram = place(gram, k, count - 1, step_of(k), last)
+    gram = place(gram, count - 1, count - 1, last, last)
+    grams[me] = gram
+    each(lambda k: gram_copy(k, me).start())
+    each(lambda k: gram_copy(k, lax.rem(me + n - k, n)).wait_recv())
+    total = lax.fori_loop(0, n, lambda d, sofar: sofar + grams[d], jnp.zeros(tile, F32))
+
+    diagonal = jnp.where(down == over, total, 0.0)
+    trace = jnp.sum(jnp.sum(diagonal, axis=0, keepdims=True), axis=1, keepdims=True)
+    ridge = 1e-06 * trace / count
+    system = jnp.where(down == over, total + ridge, total)
+    system = jnp.where(over == count, 1.0, system)
+    for k in range(count):
+        pivot = system[k:k + 1, :] / system[k:k + 1, k:k + 1]
+        system = jnp.where(down == k, pivot, system - system[:, k:k + 1] * pivot)
+    y = system[:, count:count + 1]
+    weights = y / jnp.sum(y, axis=0, keepdims=True)
+    coef_ref[...] = weights
+    result = weights[count - 1:count, :] * out_ref[...]
+    for k in range(count - 1):
+        result += weights[k:k + 1, :] * hist_ref[k + 1]
+    out_ref[...] = result
+    each(lambda k: mirror_copy(k, spot(row, col)).wait_send())
+    each(lambda k: gram_copy(k, me).wait_send())
+
+
+def finish(block, denominators, history):
     n_col = lax.axis_size("col")
     n_row = lax.axis_size("row")
-    occ_group = OCC // n_col
-    vir_group = VBLK // n_row
+    n = n_row * n_col
+    count = history.shape[0]
+    group = -(-((OCC // n_col) ** 2) // 8) * 8
+    lanes = -(-((VBLK // n_row) ** 2) // 128) * 128
+    vmem = pl.BlockSpec(memory_space=pltpu.VMEM)
+    dma = pltpu.SemaphoreType.DMA
+    return pl.pallas_call(
+        functools.partial(finish_kernel, n_row, n_col, group, lanes),
+        out_shape=(
+            jax.ShapeDtypeStruct(block.shape, F32),
+            jax.ShapeDtypeStruct((count, 1), F32),
+        ),
+        in_specs=[vmem] * 3,
+        out_specs=(vmem, vmem),
+        scratch_shapes=[
+            pltpu.VMEM((n_col * group, n_row * lanes), F32),
+            pltpu.VMEM((n_col * group, n_row * lanes), F32),
+            pltpu.VMEM((n, count, 128), F32),
+            dma((n - 1,)),
+            dma((n - 1,)),
+            dma((n - 1,)),
+            dma((n - 1,)),
+        ],
+        compiler_params=pltpu.CompilerParams(
+            collective_id=1, has_side_effects=True, vmem_limit_bytes=32 * MIB
+        ),
+    )(block, denominators, history)
+
+
+def shards(amplitudes, integrals, denominators, history):
     block = ladder_block(amplitudes, integrals)
-    shaped = block.reshape(occ_group, n_col, occ_group, vir_group, n_row, vir_group)
-    swapped = lax.all_to_all(
-        lax.all_to_all(shaped, "row", split_axis=4, concat_axis=4, tiled=True),
-        "col",
-        split_axis=1,
-        concat_axis=1,
-        tiled=True,
-    )
-    mirror_part = swapped.transpose(2, 1, 0, 5, 4, 3).reshape(block.shape)
-    symmetric = block + mirror_part
-    update = symmetric / denominators
-    following = jnp.concatenate([history[1:], update[None]], axis=0)
-    errors = following - history
-    gram = lax.psum(
-        jnp.einsum("kxy,lxy->kl", errors, errors, precision=lax.Precision.HIGHEST), ("row", "col")
-    )
-    coefficients = weights_of(gram)
-    extrapolated = jnp.einsum("k,kxy->xy", coefficients, following, precision=lax.Precision.HIGHEST)
-    return (extrapolated, coefficients)
+    extrapolated, coefficients = finish(block, denominators, history)
+    return (extrapolated, coefficients[:, 0])
 
 
 def solution(mesh):

time: 198 us -> 128 us (0.65)
  blocking collectives: 48.8 us -> 0 us
  Pallas kernels: 101 us -> 125 us
  local copies, waits for them, and re-layouts: 23.4 us -> 1.56 us
  waiting for transfers between devices: 7.28 us -> 0 us
  other arithmetic: 7.36 us -> 0.63 us
  matrix products: 4.86 us -> 0 us
  starting transfers between devices: 3.37 us -> 0 us
    psum x1 -> x0, blocking collectives: 37.8 us -> none  [shards(): lax.psum(jnp.einsum('kxy,lxy->kl', errors, errors, precision=lax.Precisio...]
    pallas_call x0 -> x1, Pallas kernels: none -> 23.8 us  [finish(): pl.pallas_call(functools.partial(finish_kernel, n_row, n_col, group, lane...]
    all_to_all x1 -> x0, blocking collectives: 11 us -> none  [shards(): lax.all_to_all(shaped, 'row', split_axis=4, concat_axis=4, tiled=True)]
    reshape x3 -> x0, local copies, waits for them, and re-layouts: 9.1 us -> none  [the longest x2 6.67 us: shards(): block.reshape(occ_group, n_col, occ_group, vir_group, n_row, vir_group)]
    unnamed x10 -> x7, local copies, waits for them, and re-layouts: 9.37 us -> 1.56 us
    all_to_all x1 -> x0, waiting for transfers between devices: 7.28 us -> none  [shards(): lax.all_to_all(lax.all_to_all(shaped, 'row', split_axis=4, concat_axis=4,...]
    dot_general x2 -> x0, matrix products: 3.98 us -> none  [the longest x1 2.5 us: shards(): jnp.einsum('kxy,lxy->kl', errors, errors, precision=lax.Precision.HIGHEST)]
    all_to_all x2 -> x0, local copies, waits for them, and re-layouts: 3.65 us -> none  [shards(): lax.all_to_all(shaped, 'row', split_axis=4, concat_axis=4, tiled=True)]
  transfers between devices with their start and end apart: 1 -> 0, of which waited for: 1 -> 0; matrix products, arithmetic and copies ran while one was open for 0% -> 0% of each run, Pallas kernels for 0% -> 0%
where the time goes in v2:
time: 128 us
  Pallas kernels  125 us (98%)
  local copies, waits for them, and re-layouts  1.56 us (1%)
    pallas_call x1, Pallas kernels, ladder_block(): pl.pallas_call(functools.partial(ladder_kernel, n_row, n_col, n_sub, kb),...  101 us
    pallas_call x1, Pallas kernels, finish(): pl.pallas_call(functools.partial(finish_kernel, n_row, n_col, group, lane...  23.8 us

profile of v2, /device:TPU:0, one launch (start us, length us, event | category | flops | bytes accessed | tf_op | source)
XLA Modules:
  0.0 127.8 jit_solution(2110360093669676341)
XLA Ops:
  0.6 0.0 copy-start
  0.6 0.0 copy-start.1
  0.7 101.2 %shard_map.59.block_ref = f32[128,256]{1,0:T(8,128)} custom-call(f32[8192,1024]{1,0:T(8,128)} %t_hbm.1, f32[8192,1024]{1,0:T(8,128)} %v_hbm.1), custom_call_target="tpu_custom_call" | custom-call | flops 51539607552 | bytes 67108864 | tf_op jit(solution)/shard_map/pallas_call | solution.py:228
  101.8 0.0 copy-done
  101.9 0.0 copy-done.1
  101.9 0.0 copy-start.2
  101.9 0.9 copy-done.2
  102.8 23.8 %shard_map.60 = (f32[128,256]{1,0:T(8,128)S(1)}, f32[8,1]{1,0:T(8,128)S(1)}) custom-call(f32[128,256]{1,0:T(8,128)S(1)} %copy-done.2, f32[128,256]{1,0:T(8,128)S(1)} %copy-done.1, f32[8,128,256]{2,1,0:T(8,128)S(1)} %copy-done), custom_call_target="tpu_custom_call" | custom-call | tf_op jit(solution)/shard_map/pallas_call | solution.py:406
  126.6 0.6 reduce
  127.2 0.7 copy.7
Async XLA Ops:
  0.6 101.2 %copy-start = (f32[8,128,256]{2,1,0:T(8,128)S(1)}, f32[8,128,256]{2,1,0:T(8,128)}, u32[]{:S(2)}) copy-start(f32[8,128,256]{2,1,0:T(8,128)} %hist_ref.1) | copy-start | bytes 3145732
  0.6 101.2 %copy-start.1 = (f32[128,256]{1,0:T(8,128)S(1)}, f32[128,256]{1,0:T(8,128)}, u32[]{:S(2)}) copy-start(f32[128,256]{1,0:T(8,128)} %den_ref.1) | copy-start | bytes 393220
  101.9 0.9 copy-start.2
